TPU v7x, 32 devices: a whole 2x2x4 slice. The times are simulated.
32 devices in a mesh: dp: 8 (over z, x), mp: 4 (over y, core).
Axes of the slice: x: 2, y: 2, z: 4, core: 2. Of those that a mesh axis runs over, the one named last changes fastest.
Arguments:
- frames: bfloat16 [16384, 1024], P('dp'), may hold values from -6 to 6
- clip_lengths: int32 [16, 8], P('dp'), may hold values from 0 to 250, as said below
- query_weight: bfloat16 [1024, 1024], P(None, 'mp'), may hold values from -0.1875 to 0.1875
- key_weight: bfloat16 [1024, 1024], P(None, 'mp'), may hold values from -0.1875 to 0.1875
- value_weight: bfloat16 [1024, 1024], P(None, 'mp'), may hold values from -0.1875 to 0.1875
- output_weight: bfloat16 [1024, 1024], P('mp'), may hold values from -1 to 1
- gate_weight: bfloat16 [1024, 4096], P(None, 'mp'), may hold values from -0.1875 to 0.1875
- up_weight: bfloat16 [1024, 4096], P(None, 'mp'), may hold values from -0.1875 to 0.1875
- down_weight: bfloat16 [4096, 1024], P('mp'), may hold values from -0.09375 to 0.09375
- attn_gain: float32 [1024], replicated, may hold values from 0.1 to 1.9
- attn_bias: float32 [1024], replicated, may hold values from -1.2 to 1.2
- mlp_gain: float32 [1024], replicated, may hold values from 0.1 to 1.9
- mlp_bias: float32 [1024], replicated, may hold values from -1.2 to 1.2
- attn_scale: float32 [1024], replicated, may hold values from 0.5 to 2
- mlp_scale: float32 [1024], replicated, may hold values from 0.5 to 2
- cotangent: bfloat16 [16384, 1024], P('dp'), may hold values from -6 to 6
Outputs:
- out_frames: bfloat16 [16384, 1024], P('dp')
- frames_grad: bfloat16 [16384, 1024], P('dp')
- query_weight_grad: float32 [1024, 1024], P('dp', 'mp')
- key_weight_grad: float32 [1024, 1024], P('dp', 'mp')
- value_weight_grad: float32 [1024, 1024], P('dp', 'mp')
- output_weight_grad: float32 [1024, 1024], P('mp', 'dp')
- gate_weight_grad: float32 [1024, 4096], P('dp', 'mp')
- up_weight_grad: float32 [1024, 4096], P('dp', 'mp')
- down_weight_grad: float32 [4096, 1024], P('mp', 'dp')
- attn_gain_grad: float32 [1024], P('dp')
- attn_bias_grad: float32 [1024], P('dp')
- mlp_gain_grad: float32 [1024], P('dp')
- mlp_bias_grad: float32 [1024], P('dp')
- attn_scale_grad: float32 [1024], P('dp')
- mlp_scale_grad: float32 [1024], P('dp')
Inputs may be any that keep to these rules, and one draw needn't show every extreme that they name: `clip_lengths`: each entry is 0, 125 or 250; the first entry of every row is 250; the entries of a row sum to at most 1024; the frames of a row past that sum form one more segment.
All inputs are finite; a program needn't handle non-finite values.
Results may differ from a plain program's by a relative error of at most 0.02.
Values may be sent and summed in bfloat16 or wider, within the bound.
A program may use at most 192 MiB of HBM per device.

v0:
```python
import jax
import jax.numpy as jnp
from jax import lax
from jax.sharding import PartitionSpec as P

HEAD_DIM = 64
WINDOW = 128
ROW_LEN = 1024
BLOCK = 512


def product(left, right, left_dim, right_dim):
    return lax.dot_general(
        left, right, (((left_dim,), (right_dim,)), ((), ())), preferred_element_type=jnp.float32
    )


def clip_layout(lengths):
    ends = jnp.cumsum(lengths, axis=-1)
    frame_ids = jnp.arange(ROW_LEN, dtype=jnp.int32)
    passed = (frame_ids[None, :, None] >= ends[:, None, :]).astype(jnp.int32)
    segment = jnp.sum(passed, axis=-1)
    start_ids = jnp.sum(passed * lengths[:, None, :], axis=-1)
    return (segment, frame_ids[None, :] - start_ids)


def rotary_tables(position):
    half_dim = HEAD_DIM // 2
    inverse = 10000.0 ** (-jnp.arange(half_dim, dtype=jnp.float32) / half_dim)
    angle = position.astype(jnp.float32)[:, None] * inverse[None, :]
    cosine = jnp.concatenate([jnp.cos(angle), jnp.cos(angle)], -1)
    sine = jnp.concatenate([jnp.sin(angle), jnp.sin(angle)], -1)
    return (cosine, sine)


def rotate(field, cosine, sine, direction):
    half_dim = field.shape[-1] // 2
    turned = jnp.concatenate([-field[..., half_dim:], field[..., :half_dim]], -1)
    return field * cosine[:, None, :] + direction * turned * sine[:, None, :]


def normalize(source, gain_vec, bias_vec):
    centre = jnp.mean(source, -1, keepdims=True)
    centred = source - centre
    spread = lax.rsqrt(jnp.mean(centred * centred, -1, keepdims=True) + 1e-05)
    unit_val = centred * spread
    return (unit_val * gain_vec + bias_vec, unit_val, spread)


def normalize_back(grad_in, unit_val, spread, gain_vec):
    scaled = grad_in * gain_vec
    inner = (
        scaled
        - jnp.mean(scaled, -1, keepdims=True)
        - unit_val * jnp.mean(scaled * unit_val, -1, keepdims=True)
    )
    return (inner * spread, jnp.sum(grad_in * unit_val, 0), jnp.sum(grad_in, 0))


def band_mask():
    row_ids = jnp.arange(BLOCK)[:, None]
    col_ids = jnp.arange(BLOCK + WINDOW)[None, :]
    return (col_ids > row_ids) & (col_ids <= row_ids + WINDOW)


def query_blocks(field):
    return field.reshape((field.shape[0] // BLOCK, BLOCK) + field.shape[1:])


def key_blocks(field, fill_value):
    row_count = field.shape[0] // ROW_LEN
    shaped = field.reshape((row_count, ROW_LEN) + field.shape[1:])
    widths = [(0, 0), (WINDOW, 0)] + [(0, 0)] * (field.ndim - 1)
    padded = jnp.pad(shaped, widths, constant_values=fill_value)
    block_count = ROW_LEN // BLOCK
    pieces = jnp.stack(
        [
            padded[:, index_b * BLOCK : index_b * BLOCK + BLOCK + WINDOW]
            for index_b in range(block_count)
        ],
        1,
    )
    return pieces.reshape((row_count * block_count, BLOCK + WINDOW) + field.shape[1:])


def key_blocks_back(extended):
    block_count = ROW_LEN // BLOCK
    row_count = extended.shape[0] // block_count
    trailing = extended.shape[2:]
    shaped = extended.reshape((row_count, block_count) + extended.shape[1:])
    own_part = shaped[:, :, WINDOW:]
    tail_part = shaped[:, 1:, :WINDOW]
    filler = jnp.zeros((row_count, block_count - 1, BLOCK - WINDOW) + trailing, extended.dtype)
    later = jnp.concatenate([filler, tail_part], 2)
    closing = jnp.zeros((row_count, 1, BLOCK) + trailing, extended.dtype)
    own_part = own_part + jnp.concatenate([later, closing], 1)
    return own_part.reshape((row_count * ROW_LEN,) + trailing)


def masked_logits(query_blk, key_blk, seg_query, seg_key, band):
    raw_scores = jnp.einsum("qhd,khd->hqk", query_blk, key_blk, preferred_element_type=jnp.float32)
    allowed = band & (seg_query[:, None] == seg_key[None, :])
    return jnp.where(allowed[None], raw_scores * HEAD_DIM ** (-0.5), -1e30)


def attend(query_blk, key_blk, value_blk, seg_query, seg_key, band):
    logits = masked_logits(query_blk, key_blk, seg_query, seg_key, band)
    highest = jnp.max(logits, -1, keepdims=True)
    expo = jnp.exp(logits - highest)
    summed = jnp.sum(expo, -1, keepdims=True)
    weights = (expo / summed).astype(jnp.bfloat16)
    result = jnp.einsum("hqk,khd->qhd", weights, value_blk, preferred_element_type=jnp.float32)
    return (result, (highest + jnp.log(summed))[..., 0])


def attend_back(query_blk, key_blk, value_blk, seg_query, seg_key, log_total, grad_blk, band):
    logits = masked_logits(query_blk, key_blk, seg_query, seg_key, band)
    probs = jnp.exp(logits - log_total[..., None])
    low_probs = probs.astype(jnp.bfloat16)
    grad_value = jnp.einsum("hqk,qhd->khd", low_probs, grad_blk, preferred_element_type=jnp.float32)
    grad_probs = jnp.einsum("qhd,khd->hqk", grad_blk, value_blk, preferred_element_type=jnp.float32)
    inner = jnp.sum(probs * grad_probs, -1, keepdims=True)
    grad_logits = (probs * (grad_probs - inner) * HEAD_DIM ** (-0.5)).astype(jnp.bfloat16)
    grad_query = jnp.einsum(
        "hqk,khd->qhd", grad_logits, key_blk, preferred_element_type=jnp.float32
    )
    grad_key = jnp.einsum(
        "hqk,qhd->khd", grad_logits, query_blk, preferred_element_type=jnp.float32
    )
    return (grad_query, grad_key, grad_value)


def rounded(field):
    return lax.optimization_barrier(field.astype(jnp.bfloat16)).astype(jnp.float32)


def per_device(
    frames,
    clip_lengths,
    query_weight,
    key_weight,
    value_weight,
    output_weight,
    gate_weight,
    up_weight,
    down_weight,
    attn_gain,
    attn_bias,
    mlp_gain,
    mlp_bias,
    attn_scale,
    mlp_scale,
    cotangent,
):
    frame_count = frames.shape[0]
    local_heads = query_weight.shape[1] // HEAD_DIM
    segment, position = clip_layout(clip_lengths)
    segment = segment.reshape(frame_count)
    position = position.reshape(frame_count)
    cosine, sine = rotary_tables(position)
    band = band_mask()
    source = frames.astype(jnp.float32)
    normed_attn, unit_attn, spread_attn = normalize(source, attn_gain, attn_bias)
    low_attn = normed_attn.astype(jnp.bfloat16)
    query_pre = jnp.dot(low_attn, query_weight, preferred_element_type=jnp.float32).reshape(
        frame_count, local_heads, HEAD_DIM
    )
    key_pre = jnp.dot(low_attn, key_weight, preferred_element_type=jnp.float32).reshape(
        frame_count, local_heads, HEAD_DIM
    )
    query = rotate(query_pre, cosine, sine, 1.0).astype(jnp.bfloat16)
    keys = rotate(key_pre, cosine, sine, 1.0).astype(jnp.bfloat16)
    values = (
        jnp.dot(low_attn, value_weight, preferred_element_type=jnp.float32)
        .astype(jnp.bfloat16)
        .reshape(frame_count, local_heads, HEAD_DIM)
    )
    query_blk = query_blocks(query)
    key_blk = key_blocks(keys, 0.0)
    value_blk = key_blocks(values, 0.0)
    seg_query = query_blocks(segment)
    seg_key = key_blocks(segment, -1)

    def forward_item(element):
        return attend(element[0], element[1], element[2], element[3], element[4], band)

    outputs, log_totals = lax.map(forward_item, (query_blk, key_blk, value_blk, seg_query, seg_key))
    attended = outputs.reshape(frame_count, local_heads * HEAD_DIM).astype(jnp.bfloat16)
    attn_branch = lax.psum(
        jnp.dot(attended, output_weight, preferred_element_type=jnp.float32).astype(jnp.bfloat16),
        "mp",
    ).astype(jnp.float32)
    midway = source + attn_scale * attn_branch
    normed_mlp, unit_mlp, spread_mlp = normalize(midway, mlp_gain, mlp_bias)
    low_mlp = normed_mlp.astype(jnp.bfloat16)
    gating = jnp.dot(low_mlp, gate_weight, preferred_element_type=jnp.float32)
    upward = jnp.dot(low_mlp, up_weight, preferred_element_type=jnp.float32)
    activated = jax.nn.silu(gating)
    hidden = (activated * upward).astype(jnp.bfloat16)
    mlp_branch = lax.psum(
        jnp.dot(hidden, down_weight, preferred_element_type=jnp.float32).astype(jnp.bfloat16), "mp"
    ).astype(jnp.float32)
    out_frames = (midway + mlp_scale * mlp_branch).astype(jnp.bfloat16)
    grad_out = cotangent.astype(jnp.float32)
    mlp_scale_grad = jnp.sum(grad_out * mlp_branch, 0)
    grad_mlp_branch = (mlp_scale * grad_out).astype(jnp.bfloat16)
    down_grad = product(hidden, grad_mlp_branch, 0, 0)
    grad_hidden = product(grad_mlp_branch, down_weight, 1, 1)
    sigma = jax.nn.sigmoid(gating)
    grad_gating = (grad_hidden * upward * sigma * (1.0 + gating * (1.0 - sigma))).astype(
        jnp.bfloat16
    )
    grad_upward = (grad_hidden * activated).astype(jnp.bfloat16)
    gate_grad = product(low_mlp, grad_gating, 0, 0)
    upward_grad = product(low_mlp, grad_upward, 0, 0)
    grad_normed_mlp = lax.psum(
        (product(grad_gating, gate_weight, 1, 1) + product(grad_upward, up_weight, 1, 1)).astype(
            jnp.bfloat16
        ),
        "mp",
    ).astype(jnp.float32)
    grad_mid_norm, mlp_gain_grad, mlp_bias_grad = normalize_back(
        grad_normed_mlp, unit_mlp, spread_mlp, mlp_gain
    )
    grad_midway = grad_out + grad_mid_norm
    attn_scale_grad = jnp.sum(grad_midway * attn_branch, 0)
    grad_attn_branch = (attn_scale * grad_midway).astype(jnp.bfloat16)
    output_grad = product(attended, grad_attn_branch, 0, 0)
    grad_attended = (
        product(grad_attn_branch, output_weight, 1, 1)
        .astype(jnp.bfloat16)
        .reshape(frame_count, local_heads, HEAD_DIM)
    )

    def backward_item(element):
        return attend_back(
            element[0], element[1], element[2], element[3], element[4], element[5], element[6], band
        )

    grad_query_blk, grad_key_blk, grad_value_blk = lax.map(
        backward_item,
        (
            query_blk,
            key_blk,
            value_blk,
            seg_query,
            seg_key,
            log_totals,
            query_blocks(grad_attended),
        ),
    )
    grad_query_turned = rounded(grad_query_blk.reshape(frame_count, local_heads, HEAD_DIM))
    grad_key_turned = rounded(key_blocks_back(grad_key_blk))
    grad_query = (
        rotate(grad_query_turned, cosine, sine, -1.0)
        .reshape(frame_count, local_heads * HEAD_DIM)
        .astype(jnp.bfloat16)
    )
    grad_key = (
        rotate(grad_key_turned, cosine, sine, -1.0)
        .reshape(frame_count, local_heads * HEAD_DIM)
        .astype(jnp.bfloat16)
    )
    grad_value = (
        key_blocks_back(grad_value_blk)
        .reshape(frame_count, local_heads * HEAD_DIM)
        .astype(jnp.bfloat16)
    )
    query_grad = product(low_attn, grad_query, 0, 0)
    key_grad = product(low_attn, grad_key, 0, 0)
    value_grad = product(low_attn, grad_value, 0, 0)
    grad_normed_attn = lax.psum(
        (
            product(grad_query, query_weight, 1, 1)
            + product(grad_key, key_weight, 1, 1)
            + product(grad_value, value_weight, 1, 1)
        ).astype(jnp.bfloat16),
        "mp",
    ).astype(jnp.float32)
    grad_source_norm, attn_gain_grad, attn_bias_grad = normalize_back(
        grad_normed_attn, unit_attn, spread_attn, attn_gain
    )
    frames_grad = (grad_midway + grad_source_norm).astype(jnp.bfloat16)
    all_parts = (
        lax.psum_scatter(query_grad, "dp", scatter_dimension=0, tiled=True),
        lax.psum_scatter(key_grad, "dp", scatter_dimension=0, tiled=True),
        lax.psum_scatter(value_grad, "dp", scatter_dimension=0, tiled=True),
        lax.psum_scatter(output_grad, "dp", scatter_dimension=1, tiled=True),
        lax.psum_scatter(gate_grad, "dp", scatter_dimension=0, tiled=True),
        lax.psum_scatter(upward_grad, "dp", scatter_dimension=0, tiled=True),
        lax.psum_scatter(down_grad, "dp", scatter_dimension=1, tiled=True),
        lax.psum_scatter(attn_gain_grad, "dp", scatter_dimension=0, tiled=True),
        lax.psum_scatter(attn_bias_grad, "dp", scatter_dimension=0, tiled=True),
        lax.psum_scatter(mlp_gain_grad, "dp", scatter_dimension=0, tiled=True),
        lax.psum_scatter(mlp_bias_grad, "dp", scatter_dimension=0, tiled=True),
        lax.psum_scatter(attn_scale_grad, "dp", scatter_dimension=0, tiled=True),
        lax.psum_scatter(mlp_scale_grad, "dp", scatter_dimension=0, tiled=True),
    )
    return (
        out_frames,
        frames_grad,
        all_parts[0],
        all_parts[1],
        all_parts[2],
        all_parts[3],
        all_parts[4],
        all_parts[5],
        all_parts[6],
        all_parts[7],
        all_parts[8],
        all_parts[9],
        all_parts[10],
        all_parts[11],
        all_parts[12],
    )


def solution(mesh):
    in_specs = (
        P("dp", None),
        P("dp", None),
        P(None, "mp"),
        P(None, "mp"),
        P(None, "mp"),
        P("mp", None),
        P(None, "mp"),
        P(None, "mp"),
        P("mp", None),
        P(),
        P(),
        P(),
        P(),
        P(),
        P(),
        P("dp", None),
    )
    out_specs = (
        P("dp", None),
        P("dp", None),
        P("dp", "mp"),
        P("dp", "mp"),
        P("dp", "mp"),
        P("mp", "dp"),
        P("dp", "mp"),
        P("dp", "mp"),
        P("mp", "dp"),
        P("dp"),
        P("dp"),
        P("dp"),
        P("dp"),
        P("dp"),
        P("dp"),
    )
    return jax.shard_map(
        per_device, mesh=mesh, in_specs=in_specs, out_specs=out_specs, check_vma=False
    )
```

profile of v0, /device:TPU:0, one launch (start us, length us, event | category | flops | bytes accessed | tf_op | source)
XLA Modules:
  0.0 1217.4 jit_solution(4328320128182410003)
XLA Ops:
  80.9 28.7 %while.28 = (s32[]{:T(128)}, bf16[4,512,4,64]{1,3,2,0:T(8,128)(2,1)}, f32[4,4,512]{2,1,0:T(4,128)S(1)}, bf16[4,640,4,64]{1,3,2,0:T(8,128)(2,1)S(1)}, s32[4,512]{...) while((s32[]{:T(128)}, ...), condition=%wide.region_8.9_spmd.clone, body=%wide.region_5.8_spmd.clone.sunk | while | flops 352909312 | bytes 26953392 | solution.py:187
  116.4 88.3 %all-reduce.19.cloned.1.call-done = bf16[2048,1024]{1,0:T(8,128)(2,1)} async-done(((bf16[2048,1024]{1,0:T(8,128)(2,1)}), bf16[2048,1024]{1,0:T(8,128)(2,1)}) %all-reduce.19.cloned.1.call-update) | async-done | bytes 4194320 | tf_op jit(solution)/shard_map/psum | solution.py:189
  228.6 15.3 %multiply_convert_fusion.2 = (bf16[2048,1024]{1,0:T(8,128)(2,1)}, bf16[2048,1024]{1,0:T(8,128)(2,1)}, bf16[2048,1024]{1,0:T(8,128)(2,1)}) fusion(f32[2048,1024]{1,0:T(8,128)} %fusion.131, f32[2048,1024]{1,0:T(8,128)} %fusion.132, bf16[1024,1024]{1,0:T(8,128)(2,1)S(1)} %copy-done, bf16[2048,1024]{1,0:T(8,128)(2,1)S(1)} %copy-done.11, f32[1024]{0:T(1024)S(1)} %copy-done.52), kind=kOutput, calls=%fused_computation.122 | convolution fusion | flops 4332716032 | bytes 35655680 | tf_op jit(solution)/shard_map/dot_general | solution.py:13
  268.4 74.8 %all-reduce.21.cloned.1.call-done = bf16[2048,1024]{1,0:T(8,128)(2,1)} async-done(((bf16[2048,1024]{1,0:T(8,128)(2,1)}), bf16[2048,1024]{1,0:T(8,128)(2,1)}) %all-reduce.21.cloned.1.call-update) | async-done | bytes 4194320 | tf_op jit(solution)/shard_map/psum | solution.py:216
  343.2 8.8 fusion.106
  369.9 112.5 %while.29 = (s32[]{:T(128)}, bf16[4,512,4,64]{1,3,2,0:T(8,128)(2,1)}, f32[4,640,4,64]{1,3,2,0:T(8,128)}, f32[4,640,4,64]{1,3,2,0:T(8,128)}, bf16[4,640,4,64]{1,3...) while((s32[]{:T(128)}, ...), condition=%wide.region_18.19_spmd.clone, body=%wide.region_16.18_spmd.clone.sunk | while | flops 858854656 | bytes 91599584 | solution.py:240
  380.3 8.5 fusion.216
  388.8 9.6 fusion.217
  408.4 8.4 fusion.216
  416.9 9.5 fusion.217
  444.8 9.5 fusion.217
  472.8 9.5 fusion.217
  533.9 10.1 fusion.139
  544.1 10.0 fusion.140
  554.8 10.4 fusion.109
  567.1 99.3 %all-reduce.23.cloned.1.call-done = (bf16[2048,1024]{1,0:T(8,128)(2,1)}, bf16[2048,1024]{1,0:T(8,128)(2,1)}) async-done(((bf16[2048,1024]{1,0:T(8,128)(2,1)}, bf16[2048,1024]{1,0:T(8,128)(2,1)}), (bf16[2048,1024]{1,0:T(8,128)(2,1)}, bf16[2048,1024]{1,0:T(8,128)(2,1)})) %all-reduce.23.cloned.1.call-update) | async-done | bytes 8388624 | tf_op jit(solution)/shard_map/psum | solution.py:200
  672.7 14.2 %fusion.105 = (f32[1024]{0:T(1024)S(1)}, bf16[2048,1024]{1,0:T(8,128)(2,1)}, bf16[2048,1024]{1,0:T(8,128)(2,1)}) fusion(bf16[2048,1024]{1,0:T(8,128)(2,1)} %get-tuple-element.355, bf16[2048,1024]{1,0:T(8,128)(2,1)} %param.35, f32[1024]{0:T(1024)S(1)} %copy-done.53, bf16[2048,1024]{1,0:T(8,128)(2,1)S(1)} %copy-done.9, f32[1024]{0:T(1024)S(1)} %copy-done.39, ...), kind=kLoop, calls=%fused_computation.116 | loop fusion | flops 44039168 | bytes 37797888 | tf_op jit(solution)/shard_map/reduce_sum | solution.py:205
  686.9 37.3 %all-reduce.13 = (f32[1024]{0:T(1024)S(1)}, f32[1024]{0:T(1024)S(1)}, f32[1024]{0:T(1024)S(1)}, f32[1024]{0:T(1024)S(1)}, f32[1024]{0:T(1024)S(1)}, /*index=5*/f32[1024]{0:T(1024)S(1)}) all-reduce(f32[1024]{0:T(1024)S(1)} %get-tuple-element.299, f32[1024]{0:T(1024)S(1)} %get-tuple-element.304, ...), channel_id=9, replica_groups=mesh['dp'=8,'mp'=4] {'dp'}, use_global_device_ids=true, to_apply=%region_30.31.clone | all-reduce | flops 6144 | bytes 49152
  734.3 66.6 %reduce-scatter.12.cloned.1.call-done = f32[128,256]{1,0:T(8,128)} async-done(((f32[1024,256]{1,0:T(8,128)}), f32[128,256]{1,0:T(8,128)}) %reduce-scatter.12.cloned.1.call-update) | async-done | bytes 131088 | tf_op jit(solution)/shard_map/reduce_scatter | solution.py:287
  800.9 66.4 %reduce-scatter.10.cloned.1.call-done = f32[128,256]{1,0:T(8,128)} async-done(((f32[1024,256]{1,0:T(8,128)}), f32[128,256]{1,0:T(8,128)}) %reduce-scatter.10.cloned.1.call-update) | async-done | bytes 131088 | tf_op jit(solution)/shard_map/reduce_scatter | solution.py:286
  867.3 66.9 %reduce-scatter.8.cloned.1.call-done = f32[128,256]{1,0:T(8,128)} async-done(((f32[1024,256]{1,0:T(8,128)}), f32[128,256]{1,0:T(8,128)}) %reduce-scatter.8.cloned.1.call-update) | async-done | bytes 131088 | tf_op jit(solution)/shard_map/reduce_scatter | solution.py:285
  934.2 91.2 %reduce-scatter.16.cloned.1.call-done = f32[128,1024]{1,0:T(8,128)} async-done(((f32[1024,1024]{1,0:T(8,128)}), f32[128,1024]{1,0:T(8,128)}) %reduce-scatter.16.cloned.1.call-update) | async-done | bytes 524304 | tf_op jit(solution)/shard_map/reduce_scatter | solution.py:289
  1025.3 92.5 %reduce-scatter.18.cloned.1.call-done = f32[128,1024]{1,0:T(8,128)} async-done(((f32[1024,1024]{1,0:T(8,128)}), f32[128,1024]{1,0:T(8,128)}) %reduce-scatter.18.cloned.1.call-update) | async-done | bytes 524304 | tf_op jit(solution)/shard_map/reduce_scatter | solution.py:290
  1117.8 92.3 %reduce-scatter.20.cloned.1.call-done = f32[1024,128]{1,0:T(8,128)} async-done(((f32[1024,1024]{1,0:T(8,128)}), f32[1024,128]{1,0:T(8,128)}) %reduce-scatter.20.cloned.1.call-update) | async-done | bytes 524304 | tf_op jit(solution)/shard_map/reduce_scatter | solution.py:291
  (331 shorter events, 300.8 us)
Async XLA Ops:
  7.2 221.5 %copy-start = (bf16[1024,1024]{1,0:T(8,128)(2,1)S(1)}, bf16[1024,1024]{1,0:T(8,128)(2,1)}, u32[]{:S(2)}) copy-start(bf16[1024,1024]{1,0:T(8,128)(2,1)} %param.28) | copy-start | bytes 6291460
  7.2 197.4 %all-reduce.19.cloned.1.call-start = ((), (), s32[]{:S(2)}) async-start(), calls=%async_computation.7 | async-start | bytes 8388608 | tf_op jit(solution)/shard_map/psum | solution.py:189
  7.3 12.0 copy-start.48
  9.1 12.9 %copy-start.45 = (f32[1024]{0:T(1024)S(1)}, f32[1024]{0:T(1024)}, u32[]{:S(2)}) copy-start(f32[1024]{0:T(1024)} %param.29) | copy-start | bytes 12292
  9.1 12.9 %copy-start.50 = (f32[1024]{0:T(1024)S(1)}, f32[1024]{0:T(1024)}, u32[]{:S(2)}) copy-start(f32[1024]{0:T(1024)} %param.30) | copy-start | bytes 12292
  116.3 88.4 %copy-start.39 = (f32[1024]{0:T(1024)S(1)}, f32[1024]{0:T(1024)}, u32[]{:S(2)}) copy-start(f32[1024]{0:T(1024)} %param.33) | copy-start | bytes 12292
  116.3 226.8 %all-reduce.21.cloned.1.call-start = ((), (), s32[]{:S(2)}) async-start(), calls=%async_computation.8 | async-start | bytes 8388608 | tf_op jit(solution)/shard_map/psum | solution.py:216
  257.4 409.0 %all-reduce.23.cloned.1.call-start = ((), (), s32[]{:S(2)}) async-start(), calls=%async_computation.16 | async-start | bytes 16777216 | tf_op jit(solution)/shard_map/psum | solution.py:200
  352.0 10.7 copy-start.32
  388.8 9.6 copy-start.24
  416.8 9.5 copy-start.24
  444.8 9.5 copy-start.24
  472.8 9.5 copy-start.24
  512.9 221.4 %reduce-scatter.14.cloned.1.call-start = ((), (), s32[]{:S(2)}) async-start(), calls=%async_computation.12 | async-start | bytes 1179648 | tf_op jit(solution)/shard_map/reduce_scatter | solution.py:288
  519.7 281.2 %reduce-scatter.12.cloned.1.call-start = ((), (), s32[]{:S(2)}) async-start(), calls=%async_computation.11 | async-start | bytes 1179648 | tf_op jit(solution)/shard_map/reduce_scatter | solution.py:287
  524.4 342.9 %reduce-scatter.10.cloned.1.call-start = ((), (), s32[]{:S(2)}) async-start(), calls=%async_computation.10 | async-start | bytes 1179648 | tf_op jit(solution)/shard_map/reduce_scatter | solution.py:286
  529.0 405.2 %reduce-scatter.8.cloned.1.call-start = ((), (), s32[]{:S(2)}) async-start(), calls=%async_computation.9 | async-start | bytes 1179648 | tf_op jit(solution)/shard_map/reduce_scatter | solution.py:285
  533.6 491.7 %reduce-scatter.16.cloned.1.call-start = ((), (), s32[]{:S(2)}) async-start(), calls=%async_computation.13 | async-start | bytes 4718592 | tf_op jit(solution)/shard_map/reduce_scatter | solution.py:289
  544.0 573.8 %reduce-scatter.18.cloned.1.call-start = ((), (), s32[]{:S(2)}) async-start(), calls=%async_computation.14 | async-start | bytes 4718592 | tf_op jit(solution)/shard_map/reduce_scatter | solution.py:290
  554.1 656.0 %reduce-scatter.20.cloned.1.call-start = ((), (), s32[]{:S(2)}) async-start(), calls=%async_computation.15 | async-start | bytes 4718592 | tf_op jit(solution)/shard_map/reduce_scatter | solution.py:291
  565.2 101.2 %copy-start.41 = (f32[2048]{0:T(1024)S(1)}, f32[2048]{0:T(1024)}, u32[]{:S(2)}) copy-start(f32[2048]{0:T(1024)} %copy-done.40) | copy-start | bytes 24580
  565.2 101.2 %copy-start.43 = (f32[2048]{0:T(1024)S(1)}, f32[2048]{0:T(1024)}, u32[]{:S(2)}) copy-start(f32[2048]{0:T(1024)} %copy-done.42) | copy-start | bytes 24580
  565.2 101.2 %copy-start.46 = (f32[1024]{0:T(1024)S(1)}, f32[1024]{0:T(1024)}, u32[]{:S(2)}) copy-start(f32[1024]{0:T(1024)} %param.29) | copy-start | bytes 12292
  672.7 537.5 %copy-start.1 = (bf16[1024,1024]{1,0:T(8,128)(2,1)S(1)}, bf16[1024,1024]{1,0:T(8,128)(2,1)}, u32[]{:S(2)}) copy-start(bf16[1024,1024]{1,0:T(8,128)(2,1)} %param.28) | copy-start | bytes 6291460
  (60 other events, 212.0 us)
Sparse Core Ops, SparseCore 0:
  116.4 88.1 all-reduce.18
  257.5 85.6 all-reduce.20
  513.0 153.3 all-reduce.22
  670.2 64.0 reduce-scatter.13
  738.5 62.3 reduce-scatter.11
  804.7 62.4 reduce-scatter.9
  871.6 62.4 reduce-scatter.7
  938.4 86.9 reduce-scatter.15
  1030.0 87.7 reduce-scatter.17
  1121.9 88.2 reduce-scatter.19
where the time goes:
time: 1230 us; the launch traced here: 1220 us
  waiting for transfers between devices  745 us (61%)
  matrix products  235 us (19%)
  other arithmetic  105 us (9%)
  local copies, waits for them, and re-layouts  76.5 us (6%)
  blocking collectives  37.3 us (3%)
  between operations  16.1 us (1%)
    psum x1, waiting for transfers between devices, per_device(): lax.psum(jnp.dot(hidden, down_weight, preferred_element_type=jnp.float32)...  99.3 us
    reduce_scatter x1, waiting for transfers between devices, per_device(): lax.psum_scatter(upward_grad, 'dp', scatter_dimension=0, tiled=True)  92.5 us
    reduce_scatter x1, waiting for transfers between devices, per_device(): lax.psum_scatter(down_grad, 'dp', scatter_dimension=1, tiled=True)  92.3 us
    reduce_scatter x1, waiting for transfers between devices, per_device(): lax.psum_scatter(gate_grad, 'dp', scatter_dimension=0, tiled=True)  91.2 us
    psum x1, waiting for transfers between devices, per_device(): lax.psum(jnp.dot(attended, output_weight, preferred_element_type=jnp.floa...  88.3 us
    dot_general x14, matrix products, product(): lax.dot_general(left, right, (((left_dim,), (right_dim,)), ((), ())), pre...  86.1 us
    psum x1, waiting for transfers between devices, per_device(): lax.psum((product(grad_gating, gate_weight, 1, 1) + product(grad_upward,...  74.8 us
    reduce_scatter x1, waiting for transfers between devices, per_device(): lax.psum_scatter(query_grad, 'dp', scatter_dimension=0, tiled=True)  66.9 us
  transfers between devices with their start and end apart: 10, of which 10 were waited for; matrix products, arithmetic and copies ran while one was open for 7% of the time, Pallas kernels for 0%

commit v1 on v0

--- a/solution.py
+++ b/solution.py
@@ -132,6 +132,12 @@
 
 def rounded(field):
     return lax.optimization_barrier(field.astype(jnp.bfloat16)).astype(jnp.float32)
+
+
+def scattered(field, axis, scatter_dimension, tiled):
+    return lax.psum_scatter(
+        field.astype(jnp.bfloat16), axis, scatter_dimension=scatter_dimension, tiled=tiled
+    ).astype(jnp.float32)
 
 
 def per_device(
@@ -282,13 +288,13 @@
     )
     frames_grad = (grad_midway + grad_source_norm).astype(jnp.bfloat16)
     all_parts = (
-        lax.psum_scatter(query_grad, "dp", scatter_dimension=0, tiled=True),
-        lax.psum_scatter(key_grad, "dp", scatter_dimension=0, tiled=True),
-        lax.psum_scatter(value_grad, "dp", scatter_dimension=0, tiled=True),
-        lax.psum_scatter(output_grad, "dp", scatter_dimension=1, tiled=True),
-        lax.psum_scatter(gate_grad, "dp", scatter_dimension=0, tiled=True),
-        lax.psum_scatter(upward_grad, "dp", scatter_dimension=0, tiled=True),
-        lax.psum_scatter(down_grad, "dp", scatter_dimension=1, tiled=True),
+        scattered(query_grad, "dp", scatter_dimension=0, tiled=True),
+        scattered(key_grad, "dp", scatter_dimension=0, tiled=True),
+        scattered(value_grad, "dp", scatter_dimension=0, tiled=True),
+        scattered(output_grad, "dp", scatter_dimension=1, tiled=True),
+        scattered(gate_grad, "dp", scatter_dimension=0, tiled=True),
+        scattered(upward_grad, "dp", scatter_dimension=0, tiled=True),
+        scattered(down_grad, "dp", scatter_dimension=1, tiled=True),
         lax.psum_scatter(attn_gain_grad, "dp", scatter_dimension=0, tiled=True),
         lax.psum_scatter(attn_bias_grad, "dp", scatter_dimension=0, tiled=True),
         lax.psum_scatter(mlp_gain_grad, "dp", scatter_dimension=0, tiled=True),

time: 1230 us -> 1200 us (0.976)
  waiting for transfers between devices: 745 us -> 698 us
  other arithmetic: 105 us -> 120 us
    reduce_scatter x7 -> x5, waiting for transfers between devices: 483 us -> 304 us  [scattered(): lax.psum_scatter(field.astype(jnp.bfloat16), axis, scatter_dimension=scat...]
    unnamed x10 -> x12, waiting for transfers between devices: 0.16 us -> 69.2 us
    psum x1, waiting for transfers between devices: 99.3 us -> 153 us  [per_device(): lax.psum(jnp.dot(hidden, down_weight, preferred_element_type=jnp.float32)...]
  transfers between devices with their start and end apart: 10 -> 10, of which waited for: 10 -> 9; matrix products, arithmetic and copies ran while one was open for 7% -> 8% of each run, Pallas kernels for 0% -> 0%
where the time goes in v1:
time: 1200 us; the launch traced here: 1190 us
  waiting for transfers between devices  698 us (58%)
  matrix products  230 us (19%)
  other arithmetic  120 us (10%)
  local copies, waits for them, and re-layouts  83.4 us (7%)
  blocking collectives  37.1 us (3%)
  between operations  15.9 us (1%)
    reduce_scatter x5, waiting for transfers between devices, scattered(): lax.psum_scatter(field.astype(jnp.bfloat16), axis, scatter_dimension=scat...  304 us
    psum x1, waiting for transfers between devices, per_device(): lax.psum(jnp.dot(hidden, down_weight, preferred_element_type=jnp.float32)...  153 us
    psum x1, waiting for transfers between devices, per_device(): lax.psum(jnp.dot(attended, output_weight, preferred_element_type=jnp.floa...  88.3 us
    psum x1, waiting for transfers between devices, per_device(): lax.psum((product(grad_gating, gate_weight, 1, 1) + product(grad_upward,...  83.1 us
    dot_general x14, matrix products, product(): lax.dot_general(left, right, (((left_dim,), (right_dim,)), ((), ())), pre...  75.4 us
    unnamed x12, waiting for transfers between devices  69.2 us
    unnamed x1, blocking collectives  37.1 us
    dot_general x4, matrix products, attend_back(): jnp.einsum('hqk,khd->qhd', grad_logits, key_blk, preferred_element_type=j...  36.6 us
  transfers between devices with their start and end apart: 10, of which 9 were waited for; matrix products, arithmetic and copies ran while one was open for 8% of the time, Pallas kernels for 0%

profile of v1, /device:TPU:0, one launch (start us, length us, event | category | flops | bytes accessed | tf_op | source)
XLA Modules:
  0.0 1185.4 jit_solution(5669985040109280518)
XLA Ops:
  81.2 28.5 %while.28 = (s32[]{:T(128)}, bf16[4,512,4,64]{1,3,2,0:T(8,128)(2,1)}, f32[4,4,512]{2,1,0:T(4,128)S(1)}, bf16[4,640,4,64]{1,3,2,0:T(8,128)(2,1)S(1)}, s32[4,512]{...) while((s32[]{:T(128)}, ...), condition=%wide.region_8.9_spmd.clone, body=%wide.region_5.8_spmd.clone.sunk | while | flops 352909312 | bytes 26953392 | solution.py:193
  115.9 88.3 %all-reduce.19.cloned.1.call-done = bf16[2048,1024]{1,0:T(8,128)(2,1)} async-done(((bf16[2048,1024]{1,0:T(8,128)(2,1)}), bf16[2048,1024]{1,0:T(8,128)(2,1)}) %all-reduce.19.cloned.1.call-update) | async-done | bytes 4194320 | tf_op jit(solution)/shard_map/psum | solution.py:195
  228.3 15.3 %multiply_convert_fusion.2 = (bf16[2048,1024]{1,0:T(8,128)(2,1)}, bf16[2048,1024]{1,0:T(8,128)(2,1)}, bf16[2048,1024]{1,0:T(8,128)(2,1)}) fusion(f32[2048,1024]{1,0:T(8,128)} %fusion.135, f32[2048,1024]{1,0:T(8,128)} %fusion.136, bf16[1024,1024]{1,0:T(8,128)(2,1)S(1)} %copy-done, bf16[2048,1024]{1,0:T(8,128)(2,1)S(1)} %copy-done.10, f32[1024]{0:T(1024)S(1)} %copy-done.54), kind=kOutput, calls=%fused_computation.122 | convolution fusion | flops 4332716032 | bytes 35655680 | tf_op jit(solution)/shard_map/dot_general | solution.py:13
  259.6 83.1 %all-reduce.21.cloned.1.call-done = bf16[2048,1024]{1,0:T(8,128)(2,1)} async-done(((bf16[2048,1024]{1,0:T(8,128)(2,1)}), bf16[2048,1024]{1,0:T(8,128)(2,1)}) %all-reduce.21.cloned.1.call-update) | async-done | bytes 4194320 | tf_op jit(solution)/shard_map/psum | solution.py:222
  342.7 9.2 fusion.106
  369.8 117.2 %while.29 = (s32[]{:T(128)}, bf16[4,512,4,64]{1,3,2,0:T(8,128)(2,1)}, f32[4,640,4,64]{1,3,2,0:T(8,128)}, f32[4,640,4,64]{1,3,2,0:T(8,128)}, bf16[4,640,4,64]{1,3...) while((s32[]{:T(128)}, ...), condition=%wide.region_18.19_spmd.clone, body=%wide.region_16.18_spmd.clone.sunk | while | flops 858854656 | bytes 83210928 | solution.py:246
  380.9 9.2 fusion.215
  410.1 9.1 fusion.215
  419.3 9.1 fusion.216
  439.4 9.1 fusion.215
  448.5 9.2 fusion.216
  468.7 9.2 fusion.215
  530.5 9.4 fusion.124
  543.9 9.4 convolution_convert_fusion.4
  553.4 9.4 convolution_convert_fusion.5
  581.0 40.5 %reduce-scatter.16.cloned.1.call-done = bf16[128,256]{1,0:T(8,128)(2,1)} async-done(((bf16[1024,256]{1,0:T(8,128)(2,1)}), bf16[128,256]{1,0:T(8,128)(2,1)}) %reduce-scatter.16.cloned.1.call-update) | async-done | bytes 65552 | tf_op jit(solution)/shard_map/reduce_scatter | solution.py:138
  623.0 63.3 %reduce-scatter.12.cloned.1.call-done = bf16[128,256]{1,0:T(8,128)(2,1)} async-done(((bf16[1024,256]{1,0:T(8,128)(2,1)}), bf16[128,256]{1,0:T(8,128)(2,1)}) %reduce-scatter.12.cloned.1.call-update) | async-done | bytes 65552 | tf_op jit(solution)/shard_map/reduce_scatter | solution.py:138
  687.8 63.5 %reduce-scatter.14.cloned.1.call-done = bf16[128,256]{1,0:T(8,128)(2,1)} async-done(((bf16[1024,256]{1,0:T(8,128)(2,1)}), bf16[128,256]{1,0:T(8,128)(2,1)}) %reduce-scatter.14.cloned.1.call-update) | async-done | bytes 65552 | tf_op jit(solution)/shard_map/reduce_scatter | solution.py:138
  752.8 69.0 %reduce-scatter.24.cloned.1.call-done = bf16[128,1024]{1,0:T(8,128)(2,1)} async-done(((bf16[1024,1024]{1,0:T(8,128)(2,1)}), bf16[128,1024]{1,0:T(8,128)(2,1)}) %reduce-scatter.24.cloned.1.call-update) | async-done | bytes 262160
  823.8 68.2 %reduce-scatter.20.cloned.1.call-done = bf16[128,1024]{1,0:T(8,128)(2,1)} async-done(((bf16[1024,1024]{1,0:T(8,128)(2,1)}), bf16[128,1024]{1,0:T(8,128)(2,1)}) %reduce-scatter.20.cloned.1.call-update) | async-done | bytes 262160 | tf_op jit(solution)/shard_map/reduce_scatter | solution.py:138
  893.8 68.4 %reduce-scatter.18.cloned.1.call-done = bf16[128,1024]{1,0:T(8,128)(2,1)} async-done(((bf16[1024,1024]{1,0:T(8,128)(2,1)}), bf16[128,1024]{1,0:T(8,128)(2,1)}) %reduce-scatter.18.cloned.1.call-update) | async-done | bytes 262160 | tf_op jit(solution)/shard_map/reduce_scatter | solution.py:138
  964.0 153.5 %all-reduce.23.cloned.1.call-done = (bf16[2048,1024]{1,0:T(8,128)(2,1)}, bf16[2048,1024]{1,0:T(8,128)(2,1)}) async-done(((bf16[2048,1024]{1,0:T(8,128)(2,1)}, bf16[2048,1024]{1,0:T(8,128)(2,1)}), (bf16[2048,1024]{1,0:T(8,128)(2,1)}, bf16[2048,1024]{1,0:T(8,128)(2,1)})) %all-reduce.23.cloned.1.call-update) | async-done | bytes 8388624 | tf_op jit(solution)/shard_map/psum | solution.py:206
  1123.7 14.1 %fusion.105 = (f32[1024]{0:T(1024)S(1)}, bf16[2048,1024]{1,0:T(8,128)(2,1)}, bf16[2048,1024]{1,0:T(8,128)(2,1)}) fusion(bf16[2048,1024]{1,0:T(8,128)(2,1)} %get-tuple-element.355, bf16[2048,1024]{1,0:T(8,128)(2,1)} %param.35, f32[1024]{0:T(1024)S(1)} %copy-done.54, bf16[2048,1024]{1,0:T(8,128)(2,1)S(1)} %copy-done.8, f32[1024]{0:T(1024)S(1)} %copy-done.41, ...), kind=kLoop, calls=%fused_computation.116 | loop fusion | flops 44039168 | bytes 37797888 | tf_op jit(solution)/shard_map/reduce_sum | solution.py:211
  1137.8 37.1 %all-reduce.13 = (f32[1024]{0:T(1024)S(1)}, f32[1024]{0:T(1024)S(1)}, f32[1024]{0:T(1024)S(1)}, f32[1024]{0:T(1024)S(1)}, f32[1024]{0:T(1024)S(1)}, /*index=5*/f32[1024]{0:T(1024)S(1)}) all-reduce(f32[1024]{0:T(1024)S(1)} %get-tuple-element.299, f32[1024]{0:T(1024)S(1)} %get-tuple-element.304, ...), channel_id=9, replica_groups=mesh['dp'=8,'mp'=4] {'dp'}, use_global_device_ids=true, to_apply=%region_30.31.clone | all-reduce | flops 6144 | bytes 49152
  (332 shorter events, 312.4 us)
Async XLA Ops:
  7.2 221.1 %copy-start = (bf16[1024,1024]{1,0:T(8,128)(2,1)S(1)}, bf16[1024,1024]{1,0:T(8,128)(2,1)}, u32[]{:S(2)}) copy-start(bf16[1024,1024]{1,0:T(8,128)(2,1)} %param.28) | copy-start | bytes 6291460
  7.2 197.0 %all-reduce.19.cloned.1.call-start = ((), (), s32[]{:S(2)}) async-start(), calls=%async_computation.7 | async-start | bytes 8388608 | tf_op jit(solution)/shard_map/psum | solution.py:195
  7.3 12.0 %copy-start.50 = (f32[32]{0:T(128)}, f32[32]{0:T(128)S(1)}, u32[]{:S(2)}) copy-start(f32[32]{0:T(128)S(1)} %multiply_power_fusion) | copy-start | bytes 388
  9.1 12.9 %copy-start.47 = (f32[1024]{0:T(1024)S(1)}, f32[1024]{0:T(1024)}, u32[]{:S(2)}) copy-start(f32[1024]{0:T(1024)} %param.29) | copy-start | bytes 12292
  9.1 12.9 %copy-start.52 = (f32[1024]{0:T(1024)S(1)}, f32[1024]{0:T(1024)}, u32[]{:S(2)}) copy-start(f32[1024]{0:T(1024)} %param.30) | copy-start | bytes 12292
  12.6 9.4 copy-start.42
  14.0 8.0 copy-start.44
  115.9 88.4 %copy-start.41 = (f32[1024]{0:T(1024)S(1)}, f32[1024]{0:T(1024)}, u32[]{:S(2)}) copy-start(f32[1024]{0:T(1024)} %param.33) | copy-start | bytes 12292
  115.9 226.8 %all-reduce.21.cloned.1.call-start = ((), (), s32[]{:S(2)}) async-start(), calls=%async_computation.8 | async-start | bytes 8388608 | tf_op jit(solution)/shard_map/psum | solution.py:222
  256.9 322.5 %reduce-scatter.22.cloned.1.call-start = ((), (), s32[]{:S(2)}) async-start(), calls=%async_computation.14 | async-start | bytes 589824
  342.7 9.2 copy-start.3
  342.7 9.2 copy-start.7
  342.7 9.2 copy-start.11
  494.2 127.3 %reduce-scatter.16.cloned.1.call-start = ((), (), s32[]{:S(2)}) async-start(), calls=%async_computation.11 | async-start | bytes 589824 | tf_op jit(solution)/shard_map/reduce_scatter | solution.py:138
  517.7 168.6 %reduce-scatter.12.cloned.1.call-start = ((), (), s32[]{:S(2)}) async-start(), calls=%async_computation.9 | async-start | bytes 589824 | tf_op jit(solution)/shard_map/reduce_scatter | solution.py:138
  525.7 225.7 %reduce-scatter.14.cloned.1.call-start = ((), (), s32[]{:S(2)}) async-start(), calls=%async_computation.10 | async-start | bytes 589824 | tf_op jit(solution)/shard_map/reduce_scatter | solution.py:138
  530.0 291.8 %reduce-scatter.24.cloned.1.call-start = ((), (), s32[]{:S(2)}) async-start(), calls=%async_computation.15 | async-start | bytes 2359296
  543.9 348.1 %reduce-scatter.20.cloned.1.call-start = ((), (), s32[]{:S(2)}) async-start(), calls=%async_computation.13 | async-start | bytes 2359296 | tf_op jit(solution)/shard_map/reduce_scatter | solution.py:138
  553.4 408.8 %reduce-scatter.18.cloned.1.call-start = ((), (), s32[]{:S(2)}) async-start(), calls=%async_computation.12 | async-start | bytes 2359296 | tf_op jit(solution)/shard_map/reduce_scatter | solution.py:138
  562.9 554.6 %all-reduce.23.cloned.1.call-start = ((), (), s32[]{:S(2)}) async-start(), calls=%async_computation.16 | async-start | bytes 16777216 | tf_op jit(solution)/shard_map/psum | solution.py:206
  563.1 8.3 copy-start.36
  577.5 539.9 %copy-start.43 = (f32[2048]{0:T(1024)S(1)}, f32[2048]{0:T(1024)}, u32[]{:S(2)}) copy-start(f32[2048]{0:T(1024)} %copy-done.42) | copy-start | bytes 24580
  577.5 539.9 %copy-start.45 = (f32[2048]{0:T(1024)S(1)}, f32[2048]{0:T(1024)}, u32[]{:S(2)}) copy-start(f32[2048]{0:T(1024)} %copy-done.44) | copy-start | bytes 24580
  577.5 539.9 %copy-start.48 = (f32[1024]{0:T(1024)S(1)}, f32[1024]{0:T(1024)}, u32[]{:S(2)}) copy-start(f32[1024]{0:T(1024)} %param.29) | copy-start | bytes 12292
  (55 other events, 174.1 us)
Sparse Core Ops, SparseCore 0:
  116.0 88.1 all-reduce.18
  257.0 85.6 all-reduce.20
  494.3 62.0 reduce-scatter.21
  560.5 60.9 reduce-scatter.15
  625.3 60.9 reduce-scatter.11
  690.4 60.8 reduce-scatter.13
  754.8 66.9 reduce-scatter.23
  825.4 66.5 reduce-scatter.19
  895.6 66.5 reduce-scatter.17
  965.2 152.2 all-reduce.22
